TPU v7x, 32 devices: a whole 2x2x4 slice. The times are simulated.
32 devices in a mesh: island: 2 (over core), fsdp: 4 (over z), tensor: 4 (over y, x).
Axes of the slice: x: 2, y: 2, z: 4, core: 2. Of those that a mesh axis runs over, the one named last changes fastest.
Arguments:
- tokens: bfloat16 [2048, 4608], P(('island', 'fsdp')), may hold values from -6 to 6
- cotangent: bfloat16 [2048, 4608], P(('island', 'fsdp')), may hold values from -0.19921875 to 0.19921875
- gate_tiles: bfloat16 [16, 4, 128, 128], P('fsdp', 'tensor'), may hold values from -1 to 1
- up_tiles: bfloat16 [16, 4, 128, 128], P('fsdp', 'tensor'), may hold values from -1 to 1
- gate_where: int32 [16, 4], P('fsdp', 'tensor'), may hold values from 0 to 2591, as said below
- up_where: int32 [16, 4], P('fsdp', 'tensor'), may hold values from 0 to 2591, as said below
- down_where: int32 [16, 4], P(None, 'tensor'), may hold values from 0 to 2591, as said below
- down_global: float32 [16, 4, 128, 128], P('fsdp', 'tensor'), may hold values from -6 to 6
- down_moment: float32 [16, 4, 128, 128], P('fsdp', 'tensor'), may hold values from -3 to 3
Outputs:
- new_global: float32 [16, 4, 128, 128], P('fsdp', 'tensor')
- new_moment: float32 [16, 4, 128, 128], P('fsdp', 'tensor')
Inputs may be any that keep to these rules, and one draw needn't show every extreme that they name: In each column t, the 16 entries of gate_where are distinct cells r * 72 + c of the 36 x 72 tile grid of shard t (r a block of the model width, c a block of the shard's hidden units). In each column t, the 16 entries of up_where are distinct cells r * 72 + c of the 36 x 72 tile grid of shard t. In each column t, the 16 entries of down_where are distinct cells a * 36 + b, a a block of shard t's hidden units (72 of them) and b a block of the model width.
All inputs are finite; a program needn't handle non-finite values.
Results may differ from a plain program's by a relative error of at most 0.00057.
Values may be sent and summed in bfloat16 or wider, within the bound.
A program may use at most 128 MiB of HBM per device.

v0:
```python
import jax
import jax.numpy as jnp
from jax import lax
from jax.sharding import PartitionSpec as P

FF = 36864


inner_rate = 0.5
decay_rate = 0.1
outer_rate = 0.7
momentum_rate = 0.9


def merge_tiles(total, tok_blocks, tiles, where, col_blocks):
    row_ids = where // col_blocks
    col_ids = where % col_blocks
    picked = jnp.take(tok_blocks, row_ids, axis=1)
    partial_value = jnp.einsum("tkr,krc->tkc", picked, tiles, preferred_element_type=jnp.float32)
    return total.at[:, col_ids].add(partial_value)


def body(
    tokens,
    cotangent,
    gate_tiles,
    up_tiles,
    gate_where,
    up_where,
    down_where,
    down_global,
    down_moment,
):
    count_rows = tokens.shape[0]
    tile_side = gate_tiles.shape[2]
    row_blocks = tokens.shape[1] // tile_side
    col_blocks = FF // tile_side // lax.axis_size("tensor")
    tok_blocks = tokens.reshape(count_rows, row_blocks, tile_side)
    cot_blocks = cotangent.reshape(count_rows, row_blocks, tile_side)
    zero_init = jnp.zeros((count_rows, col_blocks, tile_side), jnp.float32)
    gate_piece = lax.all_gather(gate_tiles, "fsdp", axis=0, tiled=True)
    up_piece = lax.all_gather(up_tiles, "fsdp", axis=0, tiled=True)
    gate_at = lax.all_gather(gate_where, "fsdp", axis=0, tiled=True)
    up_at = lax.all_gather(up_where, "fsdp", axis=0, tiled=True)
    gate_more = merge_tiles(zero_init, tok_blocks, gate_piece[:, 0], gate_at[:, 0], col_blocks)
    up_more = merge_tiles(zero_init, tok_blocks, up_piece[:, 0], up_at[:, 0], col_blocks)
    hidden = (jax.nn.silu(gate_more) * up_more).astype(jnp.bfloat16)
    places = down_where[:, 0]
    master = down_global[:, 0]
    moment = down_moment[:, 0]
    islands = lax.axis_size("island")
    hidden_pick = jnp.take(hidden, places // row_blocks, axis=1)
    cot_pick = jnp.take(cot_blocks, places % row_blocks, axis=1)
    summed = lax.psum_scatter(
        jnp.einsum("tka,tkb->kab", hidden_pick, cot_pick, preferred_element_type=jnp.float32),
        "fsdp",
        scatter_dimension=0,
        tiled=True,
    )
    delta_step = inner_rate * (summed + decay_rate * master)
    island_total = lax.psum(delta_step, "island")
    average = island_total / islands
    fresh_moment = momentum_rate * moment + average
    fresh_master = master - outer_rate * (average + momentum_rate * fresh_moment)
    return (fresh_master[:, None], fresh_moment[:, None])


def solution(mesh):
    placed = (
        P(("island", "fsdp"), None),
        P(("island", "fsdp"), None),
        P("fsdp", "tensor", None, None),
        P("fsdp", "tensor", None, None),
        P("fsdp", "tensor"),
        P("fsdp", "tensor"),
        P(None, "tensor"),
        P("fsdp", "tensor", None, None),
        P("fsdp", "tensor", None, None),
    )
    return jax.shard_map(
        body,
        mesh=mesh,
        in_specs=placed,
        out_specs=(P("fsdp", "tensor", None, None), P("fsdp", "tensor", None, None)),
        check_vma=False,
    )
```

profile of v0, /device:TPU:11, one launch (start us, length us, event | category | flops | bytes accessed | tf_op | source)
XLA Modules:
  0.0 167.6 jit_solution(5089679177161831599)
XLA Ops:
  7.2 0.0 reduce-scatter.2.cloned.1.call-start
  7.2 1.2 dynamic-slice
  9.1 0.8 bitcast_dynamic-update-slice_fusion
  9.9 0.7 bitcast_dynamic-update-slice_fusion.1
  10.6 6.4 %all-reduce.2 = (s32[16]{0:T(128)S(1)}, s32[16]{0:T(128)S(1)}) all-reduce(s32[16]{0:T(128)S(1)} %bitcast_dynamic-update-slice_fusion, s32[16]{0:T(128)S(1)} %bitcast_dynamic-update-slice_fusion.1), channel_id=1, replica_groups=mesh['island'=2,'fsdp'=4,'tensor'=4] {'fsdp'}, use_global_device_ids=true, to_apply=%add.1 | all-reduce | flops 32 | bytes 256
  17.0 0.6 compare_and_fusion.2
  17.6 0.5 compare_and_fusion.1
  18.2 1.3 and_bitcast_fusion
  19.4 1.2 compare_and_fusion
  20.6 2.9 %copy.26 = bf16[256,4608]{0,1:T(8,128)(2,1)S(1)} copy(bf16[256,4608]{1,0:T(8,128)(2,1)} %param.11) | data formatting | bytes 4718592 | tf_op args[0]
  23.5 2.5 %copy.27 = bf16[256,36,128]{2,0,1:T(8,128)(2,1)} copy(bf16[256,36,128]{0,2,1:T(8,128)(2,1)S(1)} %bitcast.102) | data formatting | bytes 4718592 | tf_op jit(solution)/shard_map/reshape | solution.py:38
  26.0 12.2 %all_gather.13 = bf16[16,1,128,128]{3,2,1,0:T(8,128)(2,1)} all-gather(bf16[4,1,128,128]{3,2,1,0:T(8,128)(2,1)S(1)} %copy-done.2), channel_id=1, replica_groups=mesh['island'=2,'fsdp'=4,'tensor'=4] {'fsdp'}, dimensions={0}, use_global_device_ids=true | all-gather | bytes 655360 | tf_op jit(solution)/shard_map/all_gather | solution.py:41
  38.2 3.3 %gather_fusion.1 = bf16[16,256,128]{2,1,0:T(8,128)(2,1)} fusion(bf16[256,36,128]{2,0,1:T(8,128)(2,1)} %copy.27, s32[1024]{0:T(1024)S(1)} %pad_clamp_fusion.3), kind=kCustom, calls=%fused_computation.clone | custom fusion | bytes 2097216 | tf_op jit(solution)/shard_map/jit(_take)/gather | solution.py:18
  41.5 2.4 %gather_fusion.2 = bf16[16,256,128]{2,1,0:T(8,128)(2,1)S(1)} fusion(bf16[256,36,128]{2,0,1:T(8,128)(2,1)} %copy.27, s32[1024]{0:T(1024)S(1)} %pad_clamp_fusion.2), kind=kCustom, calls=%fused_computation.1.clone | custom fusion | bytes 2097216 | tf_op jit(solution)/shard_map/jit(_take)/gather | solution.py:18
  44.0 13.6 %all_gather.15 = bf16[16,1,128,128]{3,2,1,0:T(8,128)(2,1)} all-gather(bf16[4,1,128,128]{3,2,1,0:T(8,128)(2,1)S(1)} %copy-done.3), channel_id=1, replica_groups=mesh['island'=2,'fsdp'=4,'tensor'=4] {'fsdp'}, dimensions={0}, use_global_device_ids=true | all-gather | bytes 655360 | tf_op jit(solution)/shard_map/all_gather | solution.py:42
  57.6 2.8 %copy.29 = bf16[256,4608]{0,1:T(8,128)(2,1)S(1)} copy(bf16[256,4608]{1,0:T(8,128)(2,1)} %param.12) | data formatting | bytes 4718592 | tf_op args[1]
  60.4 2.5 %copy.30 = bf16[256,36,128]{2,0,1:T(8,128)(2,1)} copy(bf16[256,36,128]{0,2,1:T(8,128)(2,1)S(1)} %bitcast.103) | data formatting | bytes 4718592 | tf_op jit(solution)/shard_map/reshape | solution.py:39
  62.9 1.8 %fusion.5 = f32[16,256,128]{2,1,0:T(8,128)S(1)} fusion(bf16[16,256,128]{2,1,0:T(8,128)(2,1)} %gather_fusion.1, pred[16]{0:T(512)(128)(4,1)S(1)} %copy-done.5, bf16[16,1,128,128]{3,2,1,0:T(8,128)(2,1)} %all_gather.13), kind=kOutput, calls=%fused_computation.12 | convolution fusion | flops 134742016 | bytes 3670032 | tf_op jit(solution)/shard_map/tkr,krc->tkc/dot_general | solution.py:19
  64.8 4.8 %broadcast_in_dim.31.clone.1 = f32[256,72,128]{2,0,1:T(8,128)} broadcast(f32[]{:T(128)} %constant.72.clone.1), dimensions={} | broadcast | bytes 9437188 | tf_op jit(solution)/shard_map/broadcast_in_dim | solution.py:40
  69.6 4.5 %scatter_fusion = f32[256,72,128]{2,0,1:T(8,128)} fusion(f32[256,72,128]{2,0,1:T(8,128)} %broadcast_in_dim.31.clone.1, s32[16]{0:T(128)S(1)} %get-tuple-element.21, f32[16,256,128]{2,1,0:T(8,128)S(1)} %fusion.5), kind=kCustom, calls=%fused_computation.4 | custom fusion | flops 524288 | bytes 6291520 | tf_op jit(solution)/shard_map/scatter-add | solution.py:20
  74.1 1.5 fusion.3
  75.7 4.8 %broadcast_in_dim.31.clone = f32[256,72,128]{2,0,1:T(8,128)} broadcast(f32[]{:T(128)} %constant.72.clone.1), dimensions={} | broadcast | bytes 9437188 | tf_op jit(solution)/shard_map/broadcast_in_dim | solution.py:40
  80.4 4.5 %scatter_fusion.1 = f32[256,72,128]{2,0,1:T(8,128)} fusion(f32[256,72,128]{2,0,1:T(8,128)} %broadcast_in_dim.31.clone, s32[16]{0:T(128)S(1)} %get-tuple-element.22, f32[16,256,128]{2,1,0:T(8,128)S(1)} %fusion.3), kind=kCustom, calls=%fused_computation.5 | custom fusion | flops 524288 | bytes 6291520 | tf_op jit(solution)/shard_map/scatter-add | solution.py:20
  85.0 9.9 %multiply_convert_fusion = bf16[256,72,128]{2,0,1:T(8,128)(2,1)} fusion(f32[256,72,128]{2,0,1:T(8,128)} %scatter_fusion.1, f32[256,72,128]{2,0,1:T(8,128)} %scatter_fusion), kind=kLoop, calls=%fused_computation.6 | loop fusion | flops 14155776 | bytes 23592960 | tf_op jit(solution)/shard_map/convert_element_type | solution.py:47
  94.9 3.1 %gather_fusion = bf16[16,256,128]{2,1,0:T(8,128)(2,1)S(1)} fusion(bf16[256,72,128]{2,0,1:T(8,128)(2,1)} %multiply_convert_fusion, s32[1024]{0:T(1024)S(1)} %pad_clamp_fusion.1), kind=kCustom, calls=%fused_computation.3 | custom fusion | bytes 2097216 | tf_op jit(solution)/shard_map/jit(_take)/gather | solution.py:52
  98.0 2.4 %gather_fusion.3 = bf16[16,256,128]{2,1,0:T(8,128)(2,1)S(1)} fusion(bf16[256,36,128]{2,0,1:T(8,128)(2,1)} %copy.30, s32[1024]{0:T(1024)S(1)} %pad_clamp_fusion), kind=kCustom, calls=%fused_computation.2.clone | custom fusion | bytes 2097216 | tf_op jit(solution)/shard_map/jit(_take)/gather | solution.py:53
  100.5 1.5 fusion
  102.1 0.0 all-reduce.5.cloned.1.call-start
  102.1 34.2 %reduce-scatter.2.cloned.1.call-done = f32[4,128,128]{2,1,0:T(8,128)} async-done(((f32[16,128,128]{2,1,0:T(8,128)}), f32[4,128,128]{2,1,0:T(8,128)}) %reduce-scatter.2.cloned.1.call-update) | async-done | bytes 262160 | tf_op jit(solution)/shard_map/reduce_scatter | solution.py:54
  136.3 1.7 %fusion.21 = f32[4,128,128]{2,1,0:T(8,128)} fusion(f32[4,128,128]{2,1,0:T(8,128)} %reduce-scatter.2.cloned.1.call-done, f32[4,1,128,128]{3,2,1,0:T(8,128)S(1)} %copy-done), kind=kLoop, calls=%fused_computation.32 | loop fusion | flops 196608 | bytes 786432 | tf_op jit(solution)/shard_map/mul | solution.py:60
  138.0 21.0 %all-reduce.5.cloned.1.call-done = f32[4,128,128]{2,1,0:T(8,128)} async-done(((f32[4,128,128]{2,1,0:T(8,128)}), f32[4,128,128]{2,1,0:T(8,128)}) %all-reduce.5.cloned.1.call-update) | async-done | bytes 262160 | tf_op jit(solution)/shard_map/psum | solution.py:61
  159.0 1.8 %fusion.23 = (f32[4,1,128,128]{3,2,1,0:T(8,128)}, f32[4,1,128,128]{3,2,1,0:T(8,128)}) fusion(f32[4,128,128]{2,1,0:T(8,128)} %all-reduce.5.cloned.1.call-done, f32[4,1,128,128]{3,2,1,0:T(8,128)S(1)} %copy-done.1, f32[4,1,128,128]{3,2,1,0:T(8,128)S(1)} %copy-done), kind=kLoop, calls=%fused_computation.34 | loop fusion | flops 458752 | bytes 1310720
  (25 shorter events, 0.1 us)
Async XLA Ops:
  7.2 129.1 %reduce-scatter.2.cloned.1.call-start = ((), (), s32[]{:S(2)}) async-start(), calls=%async_computation.1 | async-start | bytes 1310720 | tf_op jit(solution)/shard_map/reduce_scatter | solution.py:54
  20.6 5.4 %copy-start.2 = (bf16[4,1,128,128]{3,2,1,0:T(8,128)(2,1)S(1)}, bf16[4,1,128,128]{3,2,1,0:T(8,128)(2,1)}, u32[]{:S(2)}) copy-start(bf16[4,1,128,128]{3,2,1,0:T(8,128)(2,1)} %param.13) | copy-start | bytes 393220
  23.5 20.5 %copy-start.3 = (bf16[4,1,128,128]{3,2,1,0:T(8,128)(2,1)S(1)}, bf16[4,1,128,128]{3,2,1,0:T(8,128)(2,1)}, u32[]{:S(2)}) copy-start(bf16[4,1,128,128]{3,2,1,0:T(8,128)(2,1)} %param.14) | copy-start | bytes 393220
  57.6 5.3 %copy-start.5 = (pred[16]{0:T(512)(128)(4,1)S(1)}, pred[16]{0:T(512)(128)(4,1)}, u32[]{:S(2)}) copy-start(pred[16]{0:T(512)(128)(4,1)} %get-tuple-element.15) | copy-start | bytes 52
  69.6 4.5 %copy-start.4 = (pred[16]{0:T(512)(128)(4,1)S(1)}, pred[16]{0:T(512)(128)(4,1)}, u32[]{:S(2)}) copy-start(pred[16]{0:T(512)(128)(4,1)} %get-tuple-element.17) | copy-start | bytes 52
  85.0 15.5 %copy-start.6 = (pred[16]{0:T(512)(128)(4,1)S(1)}, pred[16]{0:T(512)(128)(4,1)}, u32[]{:S(2)}) copy-start(pred[16]{0:T(512)(128)(4,1)} %get-tuple-element.11) | copy-start | bytes 52
  85.0 15.5 %copy-start.7 = (pred[16]{0:T(512)(128)(4,1)S(1)}, pred[16]{0:T(512)(128)(4,1)}, u32[]{:S(2)}) copy-start(pred[16]{0:T(512)(128)(4,1)} %get-tuple-element.13) | copy-start | bytes 52
  94.9 41.4 %copy-start = (f32[4,1,128,128]{3,2,1,0:T(8,128)S(1)}, f32[4,1,128,128]{3,2,1,0:T(8,128)}, u32[]{:S(2)}) copy-start(f32[4,1,128,128]{3,2,1,0:T(8,128)} %param.18) | copy-start | bytes 786436
  94.9 64.1 %copy-start.1 = (f32[4,1,128,128]{3,2,1,0:T(8,128)S(1)}, f32[4,1,128,128]{3,2,1,0:T(8,128)}, u32[]{:S(2)}) copy-start(f32[4,1,128,128]{3,2,1,0:T(8,128)} %param.19) | copy-start | bytes 786436
  102.1 56.9 %all-reduce.5.cloned.1.call-start = ((), (), s32[]{:S(2)}) async-start(), calls=%async_computation.2 | async-start | bytes 524288 | tf_op jit(solution)/shard_map/psum | solution.py:61
Sparse Core Ops, SparseCore 0:
  102.2 34.0 reduce-scatter.1
  139.3 19.6 all-reduce.4
where the time goes:
time: 169 us; the launch traced here: 168 us
  waiting for transfers between devices  55.2 us (33%)
  local copies, waits for them, and re-layouts  34.3 us (20%)
  blocking collectives  32.2 us (19%)
  other arithmetic  26 us (15%)
  between operations  14.8 us (9%)
  matrix products  4.9 us (3%)
    reduce_scatter x1, waiting for transfers between devices, body(): lax.psum_scatter(jnp.einsum('tka,tkb->kab', hidden_pick, cot_pick, prefer...  34.2 us
    psum x1, waiting for transfers between devices, body(): island_total = lax.psum(delta_step, 'island')  21 us
    all_gather x1, blocking collectives, body(): up_piece = lax.all_gather(up_tiles, 'fsdp', axis=0, tiled=True)  13.6 us
    all_gather x1, blocking collectives, body(): gate_piece = lax.all_gather(gate_tiles, 'fsdp', axis=0, tiled=True)  12.2 us
    convert_element_type x1, other arithmetic, body(): hidden = (jax.nn.silu(gate_more) * up_more).astype(jnp.bfloat16)  9.9 us
    broadcast_in_dim x2, local copies, waits for them, and re-layouts, body(): zero_init = jnp.zeros((count_rows, col_blocks, tile_side), jnp.float32)  9.61 us
    scatter-add x2, other arithmetic, merge_tiles(): return total.at[:, col_ids].add(partial_value)  9.06 us
    unnamed x23, local copies, waits for them, and re-layouts  8.47 us
  transfers between devices with their start and end apart: 2, of which 2 were waited for; matrix products, arithmetic and copies ran while one was open for 0% of the time, Pallas kernels for 0%

commit v1 on v0

v1 whole, which is shorter than its diff:
```python
import functools

import jax
import jax.numpy as jnp
from jax import lax
from jax.experimental import pallas as pl
from jax.experimental.pallas import tpu as pltpu
from jax.sharding import PartitionSpec as P

FF = 36864
MESH = pl.DeviceIdType.MESH

inner_rate = 0.5
decay_rate = 0.1
outer_rate = 0.7
momentum_rate = 0.9


def steps(count, step):
    if count <= 4:
        for i in range(count):
            step(i)
    else:
        lax.fori_loop(0, count, lambda i, c: (step(i), c)[1], 0)


def arrival(i, z, n):
    close = jnp.minimum(z, n - 1 - z)
    near = jnp.where(i % 2 == 1, z - (i + 1) // 2, z + i // 2)
    far = jnp.where(z < n - 1 - z, i, n - 1 - i)
    return jnp.where(i <= 2 * close, near, far)


def departure(s, z, n):
    close = jnp.minimum(z, n - 1 - z)
    own = 2 * close + 1
    at = s + jnp.where(s >= own, 1, 0)
    side = jnp.where(at % 2 == 0, n - 1 - at // 2, (at - 1) // 2)
    side = jnp.where(z < n - 1 - z, side, n - 1 - side)
    return jnp.where(s == n - 1, z, side)


def kernel(
    n, groups, col_blocks,
    gate_at, up_at, down_at, gate_hbm, up_hbm, tok_hbm, cot_hbm,
    out_ref,
    tok, cot, w, meta, sums, own, give, take, moved, final, cross,
    meta_s, cols, rows, prev, last,
    in_sem, meta_ss, meta_rs, meta_ls, ag_ss, ag_rs, sis_ss, sis_rs,
    give_ss, give_rs, rs_ss, rs_rs, fin_ss, fin_rs, x_ss, x_rs,
):
    z = lax.axis_index("fsdp")
    isl = lax.axis_index("island")
    core = lax.rem(isl, 2)
    group = lax.div(isl, 2)
    sister = isl + 1 - 2 * core
    each = gate_hbm.shape[0]
    half = each // 2
    kept = n * each
    side = gate_hbm.shape[-1]
    row_blocks = tok_hbm.shape[1] // side

    local = [
        pltpu.make_async_copy(gate_hbm, w.at[0, z], in_sem.at[0]),
        pltpu.make_async_copy(up_hbm, w.at[1, z], in_sem.at[1]),
        pltpu.make_async_copy(tok, tok, in_sem.at[2]),
        pltpu.make_async_copy(cot, cot, in_sem.at[3]),
    ]
    local[0].start()
    local[1].start()

    barrier = pltpu.get_barrier_semaphore()
    for off in range(1, n):
        pl.semaphore_signal(barrier, inc=1, device_id={"fsdp": lax.rem(z + off, n)}, device_id_type=MESH)
    pl.semaphore_signal(barrier, inc=1, device_id={"island": sister}, device_id_type=MESH)
    for off in range(1, groups):
        peer = lax.rem(group + off, groups) * 2 + core
        pl.semaphore_signal(barrier, inc=1, device_id={"island": peer}, device_id_type=MESH)

    for b in range(row_blocks):
        pltpu.make_async_copy(
            tok_hbm.at[:, pl.ds(b * side, side)], tok.at[b], in_sem.at[2]).start()
    for b in range(row_blocks):
        pltpu.make_async_copy(
            cot_hbm.at[:, pl.ds(b * side, side)], cot.at[b], in_sem.at[3]).start()

    row_i = lax.broadcasted_iota(jnp.int32, (2 * each, side), 0)
    lane_i = lax.broadcasted_iota(jnp.int32, (2 * each, side), 1)
    packed = jnp.zeros((2 * each, side), jnp.int32)
    for q in range(2 * each):
        cell = gate_at[q, 0] if q < each else up_at[q - each, 0]
        r = lax.div(cell, col_blocks)
        c = cell - r * col_blocks
        packed = jnp.where(row_i == q, jnp.where(lane_i == 0, r, c), packed)
    meta[z] = packed
    zero = jnp.zeros(sums.shape[2:], jnp.float32)
    sums[0, kept] = zero
    sums[1, kept] = zero

    pl.semaphore_wait(barrier, n + groups - 1)

    def meta_copy(off):
        return pltpu.make_async_remote_copy(
            src_ref=meta.at[z], dst_ref=meta.at[z],
            send_sem=meta_ss.at[off], recv_sem=meta_rs.at[z],
            device_id={"fsdp": lax.rem(z + off, n)}, device_id_type=MESH)

    def meta_arrived(p):
        return pltpu.make_async_remote_copy(
            src_ref=meta.at[p], dst_ref=meta.at[p],
            send_sem=meta_ss.at[0], recv_sem=meta_rs.at[p],
            device_id={"fsdp": p}, device_id_type=MESH)

    for off in range(1, n):
        meta_copy(off).start()
    local[0].wait()
    local[1].wait()

    def line(c, sub, up):
        to = jnp.minimum(z + 1, n - 1) if up else jnp.maximum(z - 1, 0)
        part = w.at[core, c, pl.ds(sub * half, half)]
        return pltpu.make_async_remote_copy(
            src_ref=part, dst_ref=part,
            send_sem=ag_ss.at[0 if up else 1, c, sub], recv_sem=ag_rs.at[c, sub],
            device_id={"fsdp": to}, device_id_type=MESH)

    def share(c, sub, which):
        part = w.at[which, c, pl.ds(sub * half, half)]
        return pltpu.make_async_remote_copy(
            src_ref=part, dst_ref=part,
            send_sem=sis_ss.at[c, sub], recv_sem=sis_rs.at[c, sub],
            device_id={"island": sister}, device_id_type=MESH)

    for sub in range(2):
        @pl.when(z < n - 1)
        def _():
            line(z, sub, True).start()

        @pl.when(z > 0)
        def _():
            line(z, sub, False).start()

    def forward(i):
        c = arrival(i, z, n)
        for sub in range(2):
            line(c, sub, True).wait_recv()

            @pl.when((c < z) & (z < n - 1))
            def _():
                line(c, sub, True).start()

            @pl.when((c > z) & (z > 0))
            def _():
                line(c, sub, False).start()

            share(c, sub, core).start()

    def tables():
        for off in range(1, n):
            meta_arrived(lax.rem(z + off, n)).wait_recv()
        copy = pltpu.make_async_copy(meta, meta_s, meta_ls)
        copy.start()
        copy.wait()
        for m in range(2):
            def read(i):
                c = arrival(i, z, n)
                for t in range(each):
                    rows[m, i * each + t] = meta_s[c, m * each + t, 0]
                    cols[m, i * each + t] = meta_s[c, m * each + t, 1]

            steps(n, read)

            def link(i, carry):
                mine = cols[m, i]
                wanted = lax.div(down_at[i, 0], row_blocks)
                before = jnp.int32(kept)
                found = jnp.int32(kept)
                for k in range(kept):
                    there = cols[m, k]
                    before = jnp.where((there == mine) & (k < i), k, before)
                    found = jnp.where(there == wanted, k, found)
                prev[m, i] = before
                last[m, i] = found
                return carry

            lax.fori_loop(0, kept, link, 0)

    def project(i):
        c = arrival(i, z, n)
        for t in range(each):
            slot = i * each + t
            for m in range(2):
                x = tok[rows[m, slot]]
                sums[m, slot] = sums[m, prev[m, slot]] + jnp.dot(
                    x, w[m, c, t], preferred_element_type=jnp.float32)

    def gather(i):
        if n <= 4:
            if i + 1 < n:
                forward(i + 1)
        else:
            @pl.when(i + 1 < n)
            def _():
                forward(i + 1)

        if n <= 4:
            if i == 0:
                tables()
                local[2].wait()
            else:
                c = arrival(i, z, n)
                for sub in range(2):
                    share(c, sub, 1 - core).wait_recv()
        else:
            @pl.when(i == 0)
            def _():
                tables()
                local[2].wait()

            @pl.when(i > 0)
            def _():
                c = arrival(i, z, n)
                for sub in range(2):
                    share(c, sub, 1 - core).wait_recv()
        project(i)

    steps(n, gather)
    local[3].wait()

    def pair(d, u):
        return pltpu.make_async_remote_copy(
            src_ref=give.at[d, u], dst_ref=take.at[d, u],
            send_sem=give_ss.at[d, u], recv_sem=give_rs.at[d, u],
            device_id={"island": sister}, device_id_type=MESH)

    def grad(j):
        g = sums[0, last[0, j]]
        u = sums[1, last[1, j]]
        e = jnp.exp(-jnp.abs(g))
        hidden = (g * jnp.where(g >= 0, 1.0, e) / (1.0 + e) * u).astype(jnp.bfloat16)
        return lax.dot_general(
            hidden, cot[lax.rem(down_at[j, 0], row_blocks)], (((0,), (0,)), ((), ())),
            preferred_element_type=jnp.float32)

    def make(s):
        d = departure(s, z, n)
        for u in range(half):
            give[d, u] = grad(d * each + (1 - core) * half + u)
            pair(d, u).start()
        for u in range(half):
            own[d, u] = grad(d * each + core * half + u)

    def hop(d, u):
        up = jnp.where(d > z, 0, 1)
        to = jnp.where(d > z, jnp.minimum(z + 1, n - 1), jnp.maximum(z - 1, 0))
        return pltpu.make_async_remote_copy(
            src_ref=own.at[d, u], dst_ref=moved.at[up, d, u],
            send_sem=rs_ss.at[d, u], recv_sem=rs_rs.at[up, d, u],
            device_id={"fsdp": to}, device_id_type=MESH)

    def came(up, d, u):
        return pltpu.make_async_remote_copy(
            src_ref=own.at[d, u], dst_ref=moved.at[up, d, u],
            send_sem=rs_ss.at[d, u], recv_sem=rs_rs.at[up, d, u],
            device_id={"fsdp": z}, device_id_type=MESH)

    def pass_on(s):
        d = departure(s, z, n)
        up = jnp.where(d > z, 0, 1)
        middle = (z > 0) & (z < n - 1)
        for u in range(half):
            pair(d, u).wait_recv()

            @pl.when(middle)
            def _():
                came(up, d, u).wait_recv()
                own[d, u] = own[d, u] + take[d, u] + moved[up, d, u]

            @pl.when(jnp.logical_not(middle))
            def _():
                own[d, u] = own[d, u] + take[d, u]

            hop(d, u).start()

    make(0)

    def scatter(s):
        make(s + 1)
        pass_on(s)

    steps(n - 1, scatter)

    def last_hop(u):
        part = final.at[core * half + u]
        return pltpu.make_async_remote_copy(
            src_ref=part, dst_ref=part, send_sem=fin_ss.at[u], recv_sem=fin_rs.at[u],
            device_id={"island": sister}, device_id_type=MESH)

    def other_hop(u):
        part = final.at[(1 - core) * half + u]
        return pltpu.make_async_remote_copy(
            src_ref=part, dst_ref=part, send_sem=fin_ss.at[u], recv_sem=fin_rs.at[u],
            device_id={"island": sister}, device_id_type=MESH)

    def cross_hop(off, u):
        peer = lax.rem(group + off, groups) * 2 + core
        return pltpu.make_async_remote_copy(
            src_ref=cross.at[group, u], dst_ref=cross.at[group, u],
            send_sem=x_ss.at[off, u], recv_sem=x_rs.at[group, u],
            device_id={"island": peer}, device_id_type=MESH)

    def cross_came(off, u):
        there = lax.rem(group + off, groups)
        return pltpu.make_async_remote_copy(
            src_ref=cross.at[there, u], dst_ref=cross.at[there, u],
            send_sem=x_ss.at[off, u], recv_sem=x_rs.at[there, u],
            device_id={"island": there * 2 + core}, device_id_type=MESH)

    for u in range(half):
        pair(z, u).wait_recv()
        own[z, u] = own[z, u] + take[z, u]

        @pl.when(z > 0)
        def _():
            came(0, z, u).wait_recv()
            own[z, u] = own[z, u] + moved[0, z, u]

        @pl.when(z < n - 1)
        def _():
            came(1, z, u).wait_recv()
            own[z, u] = own[z, u] + moved[1, z, u]

        if groups > 1:
            cross[group, u] = own[z, u]
            for off in range(1, groups):
                cross_hop(off, u).start()
            for off in range(1, groups):
                cross_came(off, u).wait_recv()
            total = cross[0, u]
            for g in range(1, groups):
                total = total + cross[g, u]
            final[core * half + u] = total
        else:
            final[core * half + u] = own[z, u]
        last_hop(u).start()

    for u in range(half):
        other_hop(u).wait_recv()
    out_ref[...] = final[...]

    for u in range(half):
        last_hop(u).wait_send()
        for off in range(1, groups):
            cross_hop(off, u).wait_send()
    for off in range(1, n):
        meta_copy(off).wait_send()

    def drain(c):
        for sub in range(2):
            @pl.when((c <= z) & (z < n - 1))
            def _():
                line(c, sub, True).wait_send()

            @pl.when((c >= z) & (z > 0))
            def _():
                line(c, sub, False).wait_send()

            @pl.when(c != z)
            def _():
                share(c, sub, core).wait_send()
        for u in range(half):
            pair(c, u).wait_send()

            @pl.when(c != z)
            def _():
                hop(c, u).wait_send()

    steps(n, drain)


def body(
    tokens,
    cotangent,
    gate_tiles,
    up_tiles,
    gate_where,
    up_where,
    down_where,
    down_global,
    down_moment,
):
    n = lax.axis_size("fsdp")
    islands = lax.axis_size("island")
    groups = islands // 2
    each, _, side, _ = gate_tiles.shape
    half = each // 2
    kept = n * each
    count, width = tokens.shape
    col_blocks = FF // side // lax.axis_size("tensor")
    f32, bf16, i32 = jnp.float32, jnp.bfloat16, jnp.int32
    dma = pltpu.SemaphoreType.DMA
    smem = pl.BlockSpec(memory_space=pltpu.SMEM)
    anyw = pl.BlockSpec(memory_space=pl.ANY)
    summed = pl.pallas_call(
        functools.partial(kernel, n, groups, col_blocks),
        out_shape=jax.ShapeDtypeStruct((each, side, side), f32),
        in_specs=[smem] * 3 + [anyw] * 4,
        out_specs=pl.BlockSpec(memory_space=pltpu.VMEM),
        scratch_shapes=[
            pltpu.VMEM((width // side, count, side), bf16),
            pltpu.VMEM((width // side, count, side), bf16),
            pltpu.VMEM((2, n, each, side, side), bf16),
            pltpu.VMEM((n, 2 * each, side), i32),
            pltpu.VMEM((2, kept + 1, count, side), f32),
            pltpu.VMEM((n, half, side, side), f32),
            pltpu.VMEM((n, half, side, side), f32),
            pltpu.VMEM((n, half, side, side), f32),
            pltpu.VMEM((2, n, half, side, side), f32),
            pltpu.VMEM((each, side, side), f32),
            pltpu.VMEM((groups, half, side, side), f32),
            pltpu.SMEM((n, 2 * each, side), i32),
            pltpu.SMEM((2, kept), i32),
            pltpu.SMEM((2, kept), i32),
            pltpu.SMEM((2, kept), i32),
            pltpu.SMEM((2, kept), i32),
            dma((4,)),
            dma((n,)),
            dma((n,)),
            dma,
            dma((2, n, 2)),
            dma((n, 2)),
            dma((n, 2)),
            dma((n, 2)),
            dma((n, half)),
            dma((n, half)),
            dma((n, half)),
            dma((2, n, half)),
            dma((half,)),
            dma((half,)),
            dma((groups, half)),
            dma((groups, half)),
        ],
        compiler_params=pltpu.CompilerParams(
            collective_id=0, has_side_effects=True, vmem_limit_bytes=60 * 1024 * 1024
        ),
        cost_estimate=pl.CostEstimate(
            flops=6 * kept * count * side * side,
            bytes_accessed=2 * tokens.size * 2,
            transcendentals=kept * count * side,
        ),
    )(gate_where, up_where, down_where, gate_tiles[:, 0], up_tiles[:, 0], tokens, cotangent)
    master = down_global[:, 0]
    moment = down_moment[:, 0]
    average = inner_rate * (summed / islands + decay_rate * master)
    fresh_moment = momentum_rate * moment + average
    fresh_master = master - outer_rate * (average + momentum_rate * fresh_moment)
    return (fresh_master[:, None], fresh_moment[:, None])


def solution(mesh):
    placed = (
        P(("island", "fsdp"), None),
        P(("island", "fsdp"), None),
        P("fsdp", "tensor", None, None),
        P("fsdp", "tensor", None, None),
        P("fsdp", "tensor"),
        P("fsdp", "tensor"),
        P(None, "tensor"),
        P("fsdp", "tensor", None, None),
        P("fsdp", "tensor", None, None),
    )
    return jax.shard_map(
        body,
        mesh=mesh,
        in_specs=placed,
        out_specs=(P("fsdp", "tensor", None, None), P("fsdp", "tensor", None, None)),
        check_vma=False,
    )
```

time: 169 us -> 43.7 us (0.26)
  waiting for transfers between devices: 55.2 us -> 0 us
  Pallas kernels: 0 us -> 37.1 us
  blocking collectives: 32.2 us -> 0 us
  local copies, waits for them, and re-layouts: 34.3 us -> 3.97 us
  other arithmetic: 26 us -> 1.83 us
  between operations: 14.8 us -> 0.66 us
  matrix products: 4.9 us -> 0 us
    pallas_call x0 -> x1, Pallas kernels: none -> 37.1 us  [body(): pl.pallas_call(functools.partial(kernel, n, groups, col_blocks), out_shap...]
    reduce_scatter x1 -> x0, waiting for transfers between devices: 34.2 us -> none  [body(): lax.psum_scatter(jnp.einsum('tka,tkb->kab', hidden_pick, cot_pick, prefer...]
    all_gather x2 -> x0, blocking collectives: 25.8 us -> none  [the longest x1 13.6 us: body(): up_piece = lax.all_gather(up_tiles, 'fsdp', axis=0, tiled=True)]
    psum x1 -> x0, waiting for transfers between devices: 21 us -> none  [body(): island_total = lax.psum(delta_step, 'island')]
    gather x4 -> x0, local copies, waits for them, and re-layouts: 11.3 us -> none  [the longest x2 5.74 us: merge_tiles(): picked = jnp.take(tok_blocks, row_ids, axis=1)]
    convert_element_type x1 -> x0, other arithmetic: 9.9 us -> none  [body(): hidden = (jax.nn.silu(gate_more) * up_more).astype(jnp.bfloat16)]
    broadcast_in_dim x2 -> x0, local copies, waits for them, and re-layouts: 9.61 us -> none  [body(): zero_init = jnp.zeros((count_rows, col_blocks, tile_side), jnp.float32)]
    scatter-add x2 -> x0, other arithmetic: 9.06 us -> none  [merge_tiles(): return total.at[:, col_ids].add(partial_value)]
  transfers between devices with their start and end apart: 2 -> 0, of which waited for: 2 -> 0; matrix products, arithmetic and copies ran while one was open for 0% -> 0% of each run, Pallas kernels for 0% -> 0%
where the time goes in v1:
time: 43.7 us; the launch traced here: 43.5 us
  Pallas kernels  37.1 us (85%)
  local copies, waits for them, and re-layouts  3.97 us (9%)
  other arithmetic  1.83 us (4%)
  between operations  0.66 us (2%)
    pallas_call x1, Pallas kernels, body(): pl.pallas_call(functools.partial(kernel, n, groups, col_blocks), out_shap...  37.1 us
    unnamed x7, local copies, waits for them, and re-layouts  3.97 us
    unnamed x1, other arithmetic  1.83 us

profile of v1, /device:TPU:11, one launch (start us, length us, event | category | flops | bytes accessed | tf_op | source)
XLA Modules:
  0.0 43.5 jit_solution(4453164581427525094)
XLA Ops:
  0.6 1.3 %copy.11.gate_at = s32[4,1]{1,0:T(4,128)} copy(s32[4,1]{0,1:T(1,128)} %param.13) | data formatting | bytes 32 | tf_op args[4]
  1.9 1.3 %copy.12.up_at = s32[4,1]{1,0:T(4,128)} copy(s32[4,1]{0,1:T(1,128)} %param.14) | data formatting | bytes 32 | tf_op args[5]
  3.3 1.3 %copy.13.down_at = s32[16,1]{1,0:T(8,128)} copy(s32[16,1]{0,1:T(1,128)} %param.15) | data formatting | bytes 128 | tf_op args[6]
  4.6 0.0 copy-start
  4.6 0.0 copy-start.1
  4.6 37.1 %shard_map.104 = f32[4,128,128]{2,1,0:T(8,128)} custom-call(s32[4,1]{1,0:T(4,128)} %copy.11.gate_at, s32[4,1]{1,0:T(4,128)} %copy.12.up_at, s32[16,1]{1,0:T(8,128)} %copy.13.down_at, bf16[4,128,128]{2,1,0:T(8,128)(2,1)} %bitcast.41, bf16[4,128,128]{2,1,0:T(8,128)(2,1)} %bitcast.42, bf16[256,4608]{1,0:T(8,128)(2,1)} %tok_hbm.1, bf16[256,4608]{1,0:T(8,128)(2,1)} %cot_hbm.1), custom_call_target="tpu_custom_call" | custom-call | flops 402653184 | bytes 4718592 | tf_op jit(solution)/shard_map/pallas_call | solution.py:404
  41.7 0.0 copy-done
  41.7 0.0 copy-done.1
  41.7 1.8 %fusion.3 = (f32[4,1,128,128]{3,2,1,0:T(8,128)}, f32[4,1,128,128]{3,2,1,0:T(8,128)}) fusion(f32[4,1,128,128]{3,2,1,0:T(8,128)S(1)} %copy-done, f32[4,128,128]{2,1,0:T(8,128)} %shard_map.104, f32[4,1,128,128]{3,2,1,0:T(8,128)S(1)} %copy-done.1), kind=kLoop, calls=%fused_computation.7 | loop fusion | flops 655360 | bytes 1310720
Async XLA Ops:
  4.6 37.1 %copy-start = (f32[4,1,128,128]{3,2,1,0:T(8,128)S(1)}, f32[4,1,128,128]{3,2,1,0:T(8,128)}, u32[]{:S(2)}) copy-start(f32[4,1,128,128]{3,2,1,0:T(8,128)} %param.16) | copy-start | bytes 786436
  4.6 37.1 %copy-start.1 = (f32[4,1,128,128]{3,2,1,0:T(8,128)S(1)}, f32[4,1,128,128]{3,2,1,0:T(8,128)}, u32[]{:S(2)}) copy-start(f32[4,1,128,128]{3,2,1,0:T(8,128)} %param.17) | copy-start | bytes 786436

commit v2 on v1

--- a/solution.py
+++ b/solution.py
@@ -44,7 +44,7 @@
     n, groups, col_blocks,
     gate_at, up_at, down_at, gate_hbm, up_hbm, tok_hbm, cot_hbm,
     out_ref,
-    tok, cot, w, meta, sums, own, give, take, moved, final, cross,
+    tok, cot, w, meta, sums, prod, own, give, take, moved, final, cross,
     meta_s, cols, rows, prev, last,
     in_sem, meta_ss, meta_rs, meta_ls, ag_ss, ag_rs, sis_ss, sis_rs,
     give_ss, give_rs, rs_ss, rs_rs, fin_ss, fin_rs, x_ss, x_rs,
@@ -77,18 +77,11 @@
         peer = lax.rem(group + off, groups) * 2 + core
         pl.semaphore_signal(barrier, inc=1, device_id={"island": peer}, device_id_type=MESH)
 
-    for b in range(row_blocks):
-        pltpu.make_async_copy(
-            tok_hbm.at[:, pl.ds(b * side, side)], tok.at[b], in_sem.at[2]).start()
-    for b in range(row_blocks):
-        pltpu.make_async_copy(
-            cot_hbm.at[:, pl.ds(b * side, side)], cot.at[b], in_sem.at[3]).start()
-
     row_i = lax.broadcasted_iota(jnp.int32, (2 * each, side), 0)
     lane_i = lax.broadcasted_iota(jnp.int32, (2 * each, side), 1)
     packed = jnp.zeros((2 * each, side), jnp.int32)
     for q in range(2 * each):
-        cell = gate_at[q, 0] if q < each else up_at[q - each, 0]
+        cell = gate_at[0, q] if q < each else up_at[0, q - each]
         r = lax.div(cell, col_blocks)
         c = cell - r * col_blocks
         packed = jnp.where(row_i == q, jnp.where(lane_i == 0, r, c), packed)
@@ -139,6 +132,13 @@
         @pl.when(z > 0)
         def _():
             line(z, sub, False).start()
+
+    for b in range(row_blocks):
+        pltpu.make_async_copy(
+            tok_hbm.at[:, pl.ds(b * side, side)], tok.at[b], in_sem.at[2]).start()
+    for b in range(row_blocks):
+        pltpu.make_async_copy(
+            cot_hbm.at[:, pl.ds(b * side, side)], cot.at[b], in_sem.at[3]).start()
 
     def forward(i):
         c = arrival(i, z, n)
@@ -172,7 +172,7 @@
 
             def link(i, carry):
                 mine = cols[m, i]
-                wanted = lax.div(down_at[i, 0], row_blocks)
+                wanted = lax.div(down_at[0, i], row_blocks)
                 before = jnp.int32(kept)
                 found = jnp.int32(kept)
                 for k in range(kept):
@@ -187,44 +187,66 @@
 
     def project(i):
         c = arrival(i, z, n)
+        for m in range(2):
+            for t in range(each):
+                prod[m, t] = jnp.dot(
+                    tok[rows[m, i * each + t]], w[m, c, t], preferred_element_type=jnp.float32)
         for t in range(each):
             slot = i * each + t
             for m in range(2):
-                x = tok[rows[m, slot]]
-                sums[m, slot] = sums[m, prev[m, slot]] + jnp.dot(
-                    x, w[m, c, t], preferred_element_type=jnp.float32)
-
-    def gather(i):
-        if n <= 4:
-            if i + 1 < n:
+                sums[m, slot] = sums[m, prev[m, slot]] + prod[m, t]
+
+    def shared(i):
+        c = arrival(i, z, n)
+        for sub in range(2):
+            share(c, sub, 1 - core).wait_recv()
+
+    def start():
+        tables()
+        local[2].wait()
+        project(0)
+
+    middle = (z > 0) & (z < n - 1)
+    if n == 4:
+        @pl.when(middle)
+        def _():
+            for i in range(1, n - 1):
+                forward(i)
+            tables()
+            local[2].wait()
+            forward(n - 1)
+            project(0)
+            for i in range(1, n):
+                shared(i)
+                project(i)
+
+        @pl.when(jnp.logical_not(middle))
+        def _():
+            start()
+            for i in range(1, n):
+                forward(i)
+                if 1 < i < n - 1:
+                    shared(i - 1)
+                    project(i - 1)
+                if 1 < i == n - 2:
+                    shared(i)
+                    project(i)
+            shared(n - 1)
+            project(n - 1)
+    else:
+        forward(1)
+        start()
+
+        def gather(i, carry):
+            @pl.when(i + 1 < n)
+            def _():
                 forward(i + 1)
-        else:
-            @pl.when(i + 1 < n)
-            def _():
-                forward(i + 1)
-
-        if n <= 4:
-            if i == 0:
-                tables()
-                local[2].wait()
-            else:
-                c = arrival(i, z, n)
-                for sub in range(2):
-                    share(c, sub, 1 - core).wait_recv()
-        else:
-            @pl.when(i == 0)
-            def _():
-                tables()
-                local[2].wait()
-
-            @pl.when(i > 0)
-            def _():
-                c = arrival(i, z, n)
-                for sub in range(2):
-                    share(c, sub, 1 - core).wait_recv()
-        project(i)
-
-    steps(n, gather)
+
+            shared(i)
+            project(i)
+            return carry
+
+        lax.fori_loop(1, n, gather, 0)
     local[3].wait()
 
     def pair(d, u):
@@ -239,13 +261,14 @@
         e = jnp.exp(-jnp.abs(g))
         hidden = (g * jnp.where(g >= 0, 1.0, e) / (1.0 + e) * u).astype(jnp.bfloat16)
         return lax.dot_general(
-            hidden, cot[lax.rem(down_at[j, 0], row_blocks)], (((0,), (0,)), ((), ())),
+            hidden, cot[lax.rem(down_at[0, j], row_blocks)], (((0,), (0,)), ((), ())),
             preferred_element_type=jnp.float32)
 
     def make(s):
         d = departure(s, z, n)
         for u in range(half):
             give[d, u] = grad(d * each + (1 - core) * half + u)
+        for u in range(half):
             pair(d, u).start()
         for u in range(half):
             own[d, u] = grad(d * each + core * half + u)
@@ -267,7 +290,6 @@
     def pass_on(s):
         d = departure(s, z, n)
         up = jnp.where(d > z, 0, 1)
-        middle = (z > 0) & (z < n - 1)
         for u in range(half):
             pair(d, u).wait_recv()
 
@@ -281,14 +303,27 @@
                 own[d, u] = own[d, u] + take[d, u]
 
             hop(d, u).start()
-
-    make(0)
 
     def scatter(s):
         make(s + 1)
         pass_on(s)
 
-    steps(n - 1, scatter)
+    if n == 4:
+        @pl.when(middle)
+        def _():
+            for s in range(n):
+                make(s)
+            for s in range(n - 1):
+                pass_on(s)
+
+        @pl.when(jnp.logical_not(middle))
+        def _():
+            make(0)
+            for s in range(n - 1):
+                scatter(s)
+    else:
+        make(0)
+        steps(n - 1, scatter)
 
     def last_hop(u):
         part = final.at[core * half + u]
@@ -412,6 +447,7 @@
             pltpu.VMEM((2, n, each, side, side), bf16),
             pltpu.VMEM((n, 2 * each, side), i32),
             pltpu.VMEM((2, kept + 1, count, side), f32),
+            pltpu.VMEM((2, each, count, side), f32),
             pltpu.VMEM((n, half, side, side), f32),
             pltpu.VMEM((n, half, side, side), f32),
             pltpu.VMEM((n, half, side, side), f32),
@@ -448,7 +484,7 @@
             bytes_accessed=2 * tokens.size * 2,
             transcendentals=kept * count * side,
         ),
-    )(gate_where, up_where, down_where, gate_tiles[:, 0], up_tiles[:, 0], tokens, cotangent)
+    )(gate_where.T, up_where.T, down_where.T, gate_tiles[:, 0], up_tiles[:, 0], tokens, cotangent)
     master = down_global[:, 0]
     moment = down_moment[:, 0]
     average = inner_rate * (summed / islands + decay_rate * master)

time: 43.7 us -> 36.6 us (0.84)
  local copies, waits for them, and re-layouts: 3.97 us -> 0.01 us
  Pallas kernels: 37.1 us -> 33.6 us
    unnamed x7 -> x4, local copies, waits for them, and re-layouts: 3.97 us -> 0.01 us
    pallas_call x1, Pallas kernels: 37.1 us -> 33.6 us  [body(): pl.pallas_call(functools.partial(kernel, n, groups, col_blocks), out_shap...]
where the time goes in v2:
time: 36.6 us; the launch traced here: 36.1 us
  Pallas kernels  33.6 us (92%)
  other arithmetic  1.83 us (5%)
  between operations  0.67 us (2%)
    pallas_call x1, Pallas kernels, body(): pl.pallas_call(functools.partial(kernel, n, groups, col_blocks), out_shap...  33.6 us
    unnamed x1, other arithmetic  1.83 us

profile of v2, /device:TPU:11, one launch (start us, length us, event | category | flops | bytes accessed | tf_op | source)
XLA Modules:
  0.0 36.1 jit_solution(12866866283740816130)
XLA Ops:
  0.6 0.0 copy-start
  0.6 0.0 copy-start.1
  0.7 33.6 %shard_map.104 = f32[4,128,128]{2,1,0:T(8,128)} custom-call(s32[1,4]{1,0:T(1,128)} %bitcast.46, s32[1,4]{1,0:T(1,128)} %bitcast.47, s32[1,16]{1,0:T(1,128)} %bitcast.48, bf16[4,128,128]{2,1,0:T(8,128)(2,1)} %bitcast.44, bf16[4,128,128]{2,1,0:T(8,128)(2,1)} %bitcast.45, bf16[256,4608]{1,0:T(8,128)(2,1)} %tok_hbm.1, bf16[256,4608]{1,0:T(8,128)(2,1)} %cot_hbm.1), custom_call_target="tpu_custom_call" | custom-call | flops 402653184 | bytes 4718592 | tf_op jit(solution)/shard_map/pallas_call | solution.py:439
  34.2 0.0 copy-done
  34.3 0.0 copy-done.1
  34.3 1.8 %fusion.3 = (f32[4,1,128,128]{3,2,1,0:T(8,128)}, f32[4,1,128,128]{3,2,1,0:T(8,128)}) fusion(f32[4,1,128,128]{3,2,1,0:T(8,128)S(1)} %copy-done, f32[4,128,128]{2,1,0:T(8,128)} %shard_map.104, f32[4,1,128,128]{3,2,1,0:T(8,128)S(1)} %copy-done.1), kind=kLoop, calls=%fused_computation.7 | loop fusion | flops 655360 | bytes 1310720
Async XLA Ops:
  0.6 33.6 %copy-start = (f32[4,1,128,128]{3,2,1,0:T(8,128)S(1)}, f32[4,1,128,128]{3,2,1,0:T(8,128)}, u32[]{:S(2)}) copy-start(f32[4,1,128,128]{3,2,1,0:T(8,128)} %param.16) | copy-start | bytes 786436
  0.6 33.6 %copy-start.1 = (f32[4,1,128,128]{3,2,1,0:T(8,128)S(1)}, f32[4,1,128,128]{3,2,1,0:T(8,128)}, u32[]{:S(2)}) copy-start(f32[4,1,128,128]{3,2,1,0:T(8,128)} %param.17) | copy-start | bytes 786436

commit v3 on v2

--- a/solution.py
+++ b/solution.py
@@ -45,7 +45,7 @@
     gate_at, up_at, down_at, gate_hbm, up_hbm, tok_hbm, cot_hbm,
     out_ref,
     tok, cot, w, meta, sums, prod, own, give, take, moved, final, cross,
-    meta_s, cols, rows, prev, last,
+    wants, plan, plan_s,
     in_sem, meta_ss, meta_rs, meta_ls, ag_ss, ag_rs, sis_ss, sis_rs,
     give_ss, give_rs, rs_ss, rs_rs, fin_ss, fin_rs, x_ss, x_rs,
 ):
@@ -77,14 +77,13 @@
         peer = lax.rem(group + off, groups) * 2 + core
         pl.semaphore_signal(barrier, inc=1, device_id={"island": peer}, device_id_type=MESH)
 
-    row_i = lax.broadcasted_iota(jnp.int32, (2 * each, side), 0)
-    lane_i = lax.broadcasted_iota(jnp.int32, (2 * each, side), 1)
-    packed = jnp.zeros((2 * each, side), jnp.int32)
+    row_i = lax.broadcasted_iota(jnp.int32, (4 * each, side), 0)
+    packed = jnp.zeros((4 * each, side), jnp.int32)
     for q in range(2 * each):
         cell = gate_at[0, q] if q < each else up_at[0, q - each]
         r = lax.div(cell, col_blocks)
         c = cell - r * col_blocks
-        packed = jnp.where(row_i == q, jnp.where(lane_i == 0, r, c), packed)
+        packed = jnp.where(row_i == q, c, jnp.where(row_i == 2 * each + q, r, packed))
     meta[z] = packed
     zero = jnp.zeros(sums.shape[2:], jnp.float32)
     sums[0, kept] = zero
@@ -140,6 +139,13 @@
         pltpu.make_async_copy(
             cot_hbm.at[:, pl.ds(b * side, side)], cot.at[b], in_sem.at[3]).start()
 
+    lane_i = lax.broadcasted_iota(jnp.int32, plan.shape, 1)
+    row_j = lax.broadcasted_iota(jnp.int32, plan.shape, 0)
+    wanted = jnp.full(plan.shape, -1, jnp.int32)
+    for j in range(kept):
+        wanted = jnp.where(lane_i == j, lax.div(down_at[0, j], row_blocks), wanted)
+    wants[...] = wanted
+
     def forward(i):
         c = arrival(i, z, n)
         for sub in range(2):
@@ -158,43 +164,44 @@
     def tables():
         for off in range(1, n):
             meta_arrived(lax.rem(z + off, n)).wait_recv()
-        copy = pltpu.make_async_copy(meta, meta_s, meta_ls)
+        wanted = wants[...]
+        packed = jnp.zeros(plan.shape, jnp.int32)
+        for m in range(2):
+            mine = jnp.full(plan.shape, -1, jnp.int32)
+            block = jnp.zeros(plan.shape, jnp.int32)
+            there = []
+            for i in range(n):
+                got = meta[arrival(i, z, n)]
+                for t in range(each):
+                    q = m * each + t
+                    c = jnp.broadcast_to(got[q:q + 1], plan.shape)
+                    r = jnp.broadcast_to(got[2 * each + q:2 * each + q + 1], plan.shape)
+                    here = lane_i == len(there)
+                    mine = jnp.where(here, c, mine)
+                    block = jnp.where(here, r, block)
+                    there.append(c)
+            before = jnp.full(plan.shape, kept, jnp.int32)
+            found = before
+            for k in range(kept):
+                before = jnp.where((there[k] == mine) & (lane_i > k), k, before)
+                found = jnp.where(there[k] == wanted, k, found)
+            for at, value in ((m, before), (2 + m, found), (4 + m, block)):
+                packed = jnp.where(row_j == at, value, packed)
+        plan[...] = packed
+        copy = pltpu.make_async_copy(plan, plan_s, meta_ls)
         copy.start()
         copy.wait()
-        for m in range(2):
-            def read(i):
-                c = arrival(i, z, n)
-                for t in range(each):
-                    rows[m, i * each + t] = meta_s[c, m * each + t, 0]
-                    cols[m, i * each + t] = meta_s[c, m * each + t, 1]
-
-            steps(n, read)
-
-            def link(i, carry):
-                mine = cols[m, i]
-                wanted = lax.div(down_at[0, i], row_blocks)
-                before = jnp.int32(kept)
-                found = jnp.int32(kept)
-                for k in range(kept):
-                    there = cols[m, k]
-                    before = jnp.where((there == mine) & (k < i), k, before)
-                    found = jnp.where(there == wanted, k, found)
-                prev[m, i] = before
-                last[m, i] = found
-                return carry
-
-            lax.fori_loop(0, kept, link, 0)
 
     def project(i):
         c = arrival(i, z, n)
         for m in range(2):
             for t in range(each):
                 prod[m, t] = jnp.dot(
-                    tok[rows[m, i * each + t]], w[m, c, t], preferred_element_type=jnp.float32)
+                    tok[plan_s[4 + m, i * each + t]], w[m, c, t], preferred_element_type=jnp.float32)
         for t in range(each):
             slot = i * each + t
             for m in range(2):
-                sums[m, slot] = sums[m, prev[m, slot]] + prod[m, t]
+                sums[m, slot] = sums[m, plan_s[m, slot]] + prod[m, t]
 
     def shared(i):
         c = arrival(i, z, n)
@@ -210,12 +217,9 @@
     if n == 4:
         @pl.when(middle)
         def _():
-            for i in range(1, n - 1):
+            for i in range(1, n):
                 forward(i)
-            tables()
-            local[2].wait()
-            forward(n - 1)
-            project(0)
+            start()
             for i in range(1, n):
                 shared(i)
                 project(i)
@@ -256,8 +260,8 @@
             device_id={"island": sister}, device_id_type=MESH)
 
     def grad(j):
-        g = sums[0, last[0, j]]
-        u = sums[1, last[1, j]]
+        g = sums[0, plan_s[2, j]]
+        u = sums[1, plan_s[3, j]]
         e = jnp.exp(-jnp.abs(g))
         hidden = (g * jnp.where(g >= 0, 1.0, e) / (1.0 + e) * u).astype(jnp.bfloat16)
         return lax.dot_general(
@@ -287,40 +291,45 @@
             send_sem=rs_ss.at[d, u], recv_sem=rs_rs.at[up, d, u],
             device_id={"fsdp": z}, device_id_type=MESH)
 
-    def pass_on(s):
+    def pass_on(s, u):
         d = departure(s, z, n)
         up = jnp.where(d > z, 0, 1)
-        for u in range(half):
-            pair(d, u).wait_recv()
-
-            @pl.when(middle)
-            def _():
-                came(up, d, u).wait_recv()
-                own[d, u] = own[d, u] + take[d, u] + moved[up, d, u]
-
-            @pl.when(jnp.logical_not(middle))
-            def _():
-                own[d, u] = own[d, u] + take[d, u]
-
-            hop(d, u).start()
+        pair(d, u).wait_recv()
+
+        @pl.when(middle)
+        def _():
+            came(up, d, u).wait_recv()
+            own[d, u] = own[d, u] + take[d, u] + moved[up, d, u]
+
+        @pl.when(jnp.logical_not(middle))
+        def _():
+            own[d, u] = own[d, u] + take[d, u]
+
+        hop(d, u).start()
 
     def scatter(s):
         make(s + 1)
-        pass_on(s)
+        for u in range(half):
+            pass_on(s, u)
 
     if n == 4:
         @pl.when(middle)
         def _():
             for s in range(n):
                 make(s)
-            for s in range(n - 1):
-                pass_on(s)
+            for s, u in sorted(
+                ((s, u) for s in range(n - 1) for u in range(half)),
+                key=lambda p: (min(p[0], 1) + p[1] if p[0] else 0, p[0]),
+            ):
+                pass_on(s, u)
 
         @pl.when(jnp.logical_not(middle))
         def _():
-            make(0)
-            for s in range(n - 1):
-                scatter(s)
+            for s in range(n):
+                make(s)
+                if s < n - 1:
+                    for u in range(half):
+                        pass_on(s, u)
     else:
         make(0)
         steps(n - 1, scatter)
@@ -445,7 +454,7 @@
             pltpu.VMEM((width // side, count, side), bf16),
             pltpu.VMEM((width // side, count, side), bf16),
             pltpu.VMEM((2, n, each, side, side), bf16),
-            pltpu.VMEM((n, 2 * each, side), i32),
+            pltpu.VMEM((n, 4 * each, side), i32),
             pltpu.VMEM((2, kept + 1, count, side), f32),
             pltpu.VMEM((2, each, count, side), f32),
             pltpu.VMEM((n, half, side, side), f32),
@@ -454,11 +463,9 @@
             pltpu.VMEM((2, n, half, side, side), f32),
             pltpu.VMEM((each, side, side), f32),
             pltpu.VMEM((groups, half, side, side), f32),
-            pltpu.SMEM((n, 2 * each, side), i32),
-            pltpu.SMEM((2, kept), i32),
-            pltpu.SMEM((2, kept), i32),
-            pltpu.SMEM((2, kept), i32),
-            pltpu.SMEM((2, kept), i32),
+            pltpu.VMEM((8, side), i32),
+            pltpu.VMEM((8, side), i32),
+            pltpu.SMEM((8, side), i32),
             dma((4,)),
             dma((n,)),
             dma((n,)),

time: 36.6 us -> 37 us (1.011)
  no operation moved by 1% of the time
where the time goes in v3:
time: 37 us; the launch traced here: 36.2 us
  Pallas kernels  33.7 us (91%)
  other arithmetic  1.83 us (5%)
  between operations  0.67 us (2%)
    pallas_call x1, Pallas kernels, body(): pl.pallas_call(functools.partial(kernel, n, groups, col_blocks), out_shap...  33.7 us
    unnamed x1, other arithmetic  1.83 us

profile of v3, /device:TPU:11, one launch (start us, length us, event | category | flops | bytes accessed | tf_op | source)
XLA Modules:
  0.0 36.2 jit_solution(13213036716860948200)
XLA Ops:
  0.6 0.0 copy-start
  0.6 0.0 copy-start.1
  0.7 33.7 %shard_map.104 = f32[4,128,128]{2,1,0:T(8,128)} custom-call(s32[1,4]{1,0:T(1,128)} %bitcast.46, s32[1,4]{1,0:T(1,128)} %bitcast.47, s32[1,16]{1,0:T(1,128)} %bitcast.48, bf16[4,128,128]{2,1,0:T(8,128)(2,1)} %bitcast.44, bf16[4,128,128]{2,1,0:T(8,128)(2,1)} %bitcast.45, bf16[256,4608]{1,0:T(8,128)(2,1)} %tok_hbm.1, bf16[256,4608]{1,0:T(8,128)(2,1)} %cot_hbm.1), custom_call_target="tpu_custom_call" | custom-call | flops 402653184 | bytes 4718592 | tf_op jit(solution)/shard_map/pallas_call | solution.py:448
  34.4 0.0 copy-done
  34.4 0.0 copy-done.1
  34.4 1.8 %fusion.3 = (f32[4,1,128,128]{3,2,1,0:T(8,128)}, f32[4,1,128,128]{3,2,1,0:T(8,128)}) fusion(f32[4,1,128,128]{3,2,1,0:T(8,128)S(1)} %copy-done, f32[4,128,128]{2,1,0:T(8,128)} %shard_map.104, f32[4,1,128,128]{3,2,1,0:T(8,128)S(1)} %copy-done.1), kind=kLoop, calls=%fused_computation.7 | loop fusion | flops 655360 | bytes 1310720
Async XLA Ops:
  0.6 33.8 %copy-start = (f32[4,1,128,128]{3,2,1,0:T(8,128)S(1)}, f32[4,1,128,128]{3,2,1,0:T(8,128)}, u32[]{:S(2)}) copy-start(f32[4,1,128,128]{3,2,1,0:T(8,128)} %param.16) | copy-start | bytes 786436
  0.6 33.8 %copy-start.1 = (f32[4,1,128,128]{3,2,1,0:T(8,128)S(1)}, f32[4,1,128,128]{3,2,1,0:T(8,128)}, u32[]{:S(2)}) copy-start(f32[4,1,128,128]{3,2,1,0:T(8,128)} %param.17) | copy-start | bytes 786436

commit v4 on v2

--- a/solution.py
+++ b/solution.py
@@ -111,20 +111,20 @@
 
     def line(c, sub, up):
         to = jnp.minimum(z + 1, n - 1) if up else jnp.maximum(z - 1, 0)
-        part = w.at[core, c, pl.ds(sub * half, half)]
+        part = w.at[core, c, pl.ds(sub, 1)]
         return pltpu.make_async_remote_copy(
             src_ref=part, dst_ref=part,
             send_sem=ag_ss.at[0 if up else 1, c, sub], recv_sem=ag_rs.at[c, sub],
             device_id={"fsdp": to}, device_id_type=MESH)
 
     def share(c, sub, which):
-        part = w.at[which, c, pl.ds(sub * half, half)]
+        part = w.at[which, c, pl.ds(sub, 1)]
         return pltpu.make_async_remote_copy(
             src_ref=part, dst_ref=part,
             send_sem=sis_ss.at[c, sub], recv_sem=sis_rs.at[c, sub],
             device_id={"island": sister}, device_id_type=MESH)
 
-    for sub in range(2):
+    for sub in range(each):
         @pl.when(z < n - 1)
         def _():
             line(z, sub, True).start()
@@ -142,7 +142,7 @@
 
     def forward(i):
         c = arrival(i, z, n)
-        for sub in range(2):
+        for sub in range(each):
             line(c, sub, True).wait_recv()
 
             @pl.when((c < z) & (z < n - 1))
@@ -198,7 +198,7 @@
 
     def shared(i):
         c = arrival(i, z, n)
-        for sub in range(2):
+        for sub in range(each):
             share(c, sub, 1 - core).wait_recv()
 
     def start():
@@ -391,7 +391,7 @@
         meta_copy(off).wait_send()
 
     def drain(c):
-        for sub in range(2):
+        for sub in range(each):
             @pl.when((c <= z) & (z < n - 1))
             def _():
                 line(c, sub, True).wait_send()
@@ -463,10 +463,10 @@
             dma((n,)),
             dma((n,)),
             dma,
-            dma((2, n, 2)),
-            dma((n, 2)),
-            dma((n, 2)),
-            dma((n, 2)),
+            dma((2, n, each)),
+            dma((n, each)),
+            dma((n, each)),
+            dma((n, each)),
             dma((n, half)),
             dma((n, half)),
             dma((n, half)),

time: 36.6 us -> 36.9 us (level)
  Pallas kernels: 33.6 us -> 34.2 us
    pallas_call x1, Pallas kernels: 33.6 us -> 34.2 us  [body(): pl.pallas_call(functools.partial(kernel, n, groups, col_blocks), out_shap...]
where the time goes in v4:
time: 36.9 us; the launch traced here: 36.7 us
  Pallas kernels  34.2 us (93%)
  other arithmetic  1.83 us (5%)
  between operations  0.67 us (2%)
    pallas_call x1, Pallas kernels, body(): pl.pallas_call(functools.partial(kernel, n, groups, col_blocks), out_shap...  34.2 us
    unnamed x1, other arithmetic  1.83 us

profile of v4, /device:TPU:11, one launch (start us, length us, event | category | flops | bytes accessed | tf_op | source)
XLA Modules:
  0.0 36.7 jit_solution(11839254380661287540)
XLA Ops:
  0.6 0.0 copy-start
  0.6 0.0 copy-start.1
  0.7 34.2 %shard_map.104 = f32[4,128,128]{2,1,0:T(8,128)} custom-call(s32[1,4]{1,0:T(1,128)} %bitcast.46, s32[1,4]{1,0:T(1,128)} %bitcast.47, s32[1,16]{1,0:T(1,128)} %bitcast.48, bf16[4,128,128]{2,1,0:T(8,128)(2,1)} %bitcast.44, bf16[4,128,128]{2,1,0:T(8,128)(2,1)} %bitcast.45, bf16[256,4608]{1,0:T(8,128)(2,1)} %tok_hbm.1, bf16[256,4608]{1,0:T(8,128)(2,1)} %cot_hbm.1), custom_call_target="tpu_custom_call" | custom-call | flops 402653184 | bytes 4718592 | tf_op jit(solution)/shard_map/pallas_call | solution.py:439
  34.8 0.0 copy-done
  34.9 0.0 copy-done.1
  34.9 1.8 %fusion.3 = (f32[4,1,128,128]{3,2,1,0:T(8,128)}, f32[4,1,128,128]{3,2,1,0:T(8,128)}) fusion(f32[4,1,128,128]{3,2,1,0:T(8,128)S(1)} %copy-done, f32[4,128,128]{2,1,0:T(8,128)} %shard_map.104, f32[4,1,128,128]{3,2,1,0:T(8,128)S(1)} %copy-done.1), kind=kLoop, calls=%fused_computation.7 | loop fusion | flops 655360 | bytes 1310720
Async XLA Ops:
  0.6 34.2 %copy-start = (f32[4,1,128,128]{3,2,1,0:T(8,128)S(1)}, f32[4,1,128,128]{3,2,1,0:T(8,128)}, u32[]{:S(2)}) copy-start(f32[4,1,128,128]{3,2,1,0:T(8,128)} %param.16) | copy-start | bytes 786436
  0.6 34.2 %copy-start.1 = (f32[4,1,128,128]{3,2,1,0:T(8,128)S(1)}, f32[4,1,128,128]{3,2,1,0:T(8,128)}, u32[]{:S(2)}) copy-start(f32[4,1,128,128]{3,2,1,0:T(8,128)} %param.17) | copy-start | bytes 786436
